TPU v7x, 32 devices: a whole 2x2x4 slice. The times are simulated.
32 devices in a mesh: parts: 2 (over y), patch: 4 (over z), sub: 4 (over x, core).
Axes of the slice: x: 2, y: 2, z: 4, core: 2. Of those that a mesh axis runs over, the one named last changes fastest.
Arguments:
- node_latents: bfloat16 [4096, 512], P(('parts', 'patch', 'sub')), parts along dimension 0, may hold values from -6 to 6
- edge_latents: bfloat16 [16384, 512], P(('parts', 'patch', 'sub')), parts along dimension 0, may hold values from -6 to 6
- coarse_edges: bfloat16 [2048, 512], P(('parts', 'patch', 'sub')), parts along dimension 0, may hold values from -6 to 6
- w_edge_in: bfloat16 [1536, 512], replicated, may hold values from -0.15625 to 0.15625
- w_edge_out: bfloat16 [512, 512], replicated, may hold values from -0.25 to 0.25
- w_node_in: bfloat16 [1024, 512], replicated, may hold values from -0.1875 to 0.1875
- w_node_out: bfloat16 [512, 512], replicated, may hold values from -0.25 to 0.25
- fine_senders: int32 [16384], P(('parts', 'patch', 'sub')), parts along dimension 0, may hold values from 0 to 159
- fine_receivers: int32 [16384], P(('parts', 'patch', 'sub')), parts along dimension 0, may hold values from -1 to 127, as said below
- halo_lists: int32 [32, 2, 16], P(('parts', 'patch', 'sub')), parts along dimension 0, may hold values from 0 to 127, as said below
- coarse_senders: int32 [2048], P(('parts', 'patch', 'sub')), parts along dimension 0, may hold values from 0 to 63
- coarse_receivers: int32 [2048], P(('parts', 'patch', 'sub')), parts along dimension 0, may hold values from 0 to 63
Outputs:
- new_nodes: bfloat16 [4096, 512], P(('parts', 'patch', 'sub')), parts along dimension 0
- new_edges: bfloat16 [16384, 512], P(('parts', 'patch', 'sub')), parts along dimension 0
- new_coarse: bfloat16 [2048, 512], P(('parts', 'patch', 'sub')), parts along dimension 0
There are 2 independent parts, one for each index of `parts`. A program takes and returns all parts, laid end to end along the dimension named above; an argument that names none is the same for every part. Nothing has to cross between parts.
Inputs may be any that keep to these rules, and one draw needn't show every extreme that they name: `fine_receivers`: in each device's block of 512 slots the used slots come first and name a local row; the rest hold -1. At least half of a device's slots are used, and some device uses all of them. `halo_lists`: each of a device's two lists holds 16 distinct local rows.
All inputs are finite; a program needn't handle non-finite values.
Results may differ from a plain program's by a relative error of at most 0.0053.
Values may be sent and summed in bfloat16 or wider, within the bound.
No kernel may reach another device: no remote copies, remote signals or barrier semaphores. Data moves between devices by JAX's collectives and lax.ppermute only.
A program may use at most 64 MiB of HBM per device.

v0:
```python
import functools

import jax
import jax.numpy as jnp
from jax import lax
from jax.experimental import pallas as pl
from jax.experimental.pallas import tpu as pltpu
from jax.sharding import PartitionSpec as P

CO_DEV = 4
GROUP_AXES = ("patch", "sub")
TOP = 16
STEP = 128
MIB = 1 << 20
ANY = pl.BlockSpec(memory_space=pl.ANY)
VMEM = pl.BlockSpec(memory_space=pltpu.VMEM)
BF16, F32 = jnp.bfloat16, jnp.float32


def swap(value, mask, axis):
    return lax.ppermute(value, axis, [(i, i ^ mask) for i in range(lax.axis_size(axis))])


def ring_place(index, devices):
    half = devices // 2
    return 2 * (index % half) + index // half


def ring_device(place, devices):
    return (place % 2) * (devices // 2) + place // 2


def turn(value, by):
    devices = lax.axis_size("patch")
    ring = [ring_device(place, devices) for place in range(devices)]
    return lax.ppermute(value, "patch", [(ring[i], ring[(i + by) % devices]) for i in range(devices)])


def pair(value, first):
    devices = lax.axis_size(GROUP_AXES)
    pairs = [(i, (i + 1) % devices) for i in range(first, devices, 2)]
    return lax.ppermute(value, GROUP_AXES, pairs + [(b, a) for a, b in pairs])


def dot(a, b):
    return jnp.dot(a, b, preferred_element_type=F32)


def dot_t(a, b):
    return lax.dot_general(a, b, (((0,), (0,)), ((), ())), preferred_element_type=F32)


def onehot_t(rows, ids):
    at = lax.broadcasted_iota(jnp.int32, (rows, ids.shape[1]), 0)
    return jnp.where(at == ids, 1.0, 0.0).astype(BF16)


def silu(v):
    half = 0.5 * v
    return half + half * jnp.tanh(half)


def norm_parts(values):
    mean = jnp.mean(values, axis=-1, keepdims=True)
    centred = values - mean
    return centred, lax.rsqrt(jnp.mean(centred * centred, axis=-1, keepdims=True) + 1e-05)


def head_kernel(nodes_hbm, head_ref, rows_ref, sem):
    copy = pltpu.make_async_copy(nodes_hbm.at[pl.ds(0, TOP)], rows_ref, sem)
    copy.start()
    copy.wait()
    head_ref[...] = rows_ref[0:CO_DEV, :]


def join_rows(refs, order):
    refs = [refs[0]] + [ref for _, ref in sorted(zip(order, refs[1:]), key=lambda item: item[0])]
    if refs[0].shape[0] % TOP == 0:
        return jnp.concatenate([ref[...] for ref in refs], axis=0)
    return jnp.concatenate([ref[...].astype(F32) for ref in refs], axis=0).astype(BF16)


def join_kernel(masks, *refs):
    refs, (after, out_ref) = refs[:-2], refs[-2:]
    out_ref[...] = join_rows(refs, masks)


def pass_kernel(even_ref, odd_ref, after, even_out, odd_out):
    pass


def start_copies(sources, targets, sems):
    copies = [pltpu.make_async_copy(a, b, sems.at[i]) for i, (a, b) in enumerate(zip(sources, targets))]
    for copy in copies:
        copy.start()
    return copies


def load_kernel(
    nodes_hbm, lists_hbm, cedges_hbm, w_in_hbm, csend_hbm, crecv_hbm, w_out_hbm, after,
    nodes_ref, cedges_ref, w_ends_ref, w_out_ref, even_ref, odd_ref, gather_ref, picks_ref, part_ref,
    lists_ref, w_self_ref, csend_ref, crecv_ref, sems,
):
    width = nodes_ref.shape[1]
    copies = start_copies(
        [
            nodes_hbm, lists_hbm, cedges_hbm, w_in_hbm.at[pl.ds(0, width)], csend_hbm, crecv_hbm,
            w_in_hbm.at[pl.ds(width, 2 * width)], w_out_hbm,
        ],
        [nodes_ref, lists_ref, cedges_ref, w_self_ref, csend_ref, crecv_ref, w_ends_ref, w_out_ref],
        sems,
    )
    for copy in copies[:2]:
        copy.wait()
    nodes = nodes_ref[...]
    count = nodes.shape[0]
    lists = lists_ref[0]
    me = lax.axis_index(GROUP_AXES)
    odd = me % 2
    first = lists[0:1, :] * (1 - odd) + lists[1:2, :] * odd
    second = lists[1:2, :] * (1 - odd) + lists[0:1, :] * odd
    even_ref[...] = dot_t(onehot_t(count, first), nodes).astype(BF16)
    odd_ref[...] = dot_t(onehot_t(count, second), nodes).astype(BF16)
    for copy in copies[2:6]:
        copy.wait()
    part_ref[...] = dot(cedges_ref[...], w_self_ref[...])
    rows, ids = picks_ref.shape
    sub, patch = lax.axis_size("sub"), lax.axis_size("patch")
    at = lax.broadcasted_iota(jnp.int32, (rows, ids), 0)
    block = at // CO_DEV
    place = ring_place(lax.axis_index("patch"), patch) + patch - block // sub
    device = ring_device(place % patch, patch) * sub + (lax.axis_index("sub") ^ (block % sub))
    node = device * CO_DEV + at % CO_DEV
    send = jnp.where(node == csend_ref[...], 1.0, 0.0).astype(BF16)
    recv = jnp.where(node == crecv_ref[...], 1.0, 0.0).astype(BF16)
    picks_ref[...] = onehot_t(rows, crecv_ref[...])
    across = lax.broadcasted_iota(jnp.int32, (rows, rows), 0) == lax.broadcasted_iota(jnp.int32, (rows, rows), 1)
    eye = jnp.where(across, 1.0, 0.0).astype(BF16)
    gather_ref[0:ids, :] = dot_t(send, eye).astype(BF16)
    gather_ref[ids:, :] = dot_t(recv, eye).astype(BF16)
    for copy in copies[6:]:
        copy.wait()


def coarse_kernel(turns, *refs):
    parts = len(turns) + 1
    lats, refs = refs[:parts], refs[parts:]
    edges_ref, part_ref, gather_ref, picks_ref, w_ends_ref, w_out_ref, new_ref, sums_ref = refs
    count, width = edges_ref.shape
    lat = join_rows(lats, turns)
    ends = dot(gather_ref[...], lat).astype(BF16)
    ends = jnp.concatenate([ends[0:count], ends[count:]], axis=1)
    hidden = silu(part_ref[...] + dot(ends, w_ends_ref[...])).astype(BF16)
    centred, scale = norm_parts(dot(hidden, w_out_ref[...]))
    new = (edges_ref[...].astype(F32) + centred * scale).astype(BF16)
    new_ref[...] = new
    sums = dot(picks_ref[...], new).astype(BF16)
    for at in range(sums_ref.shape[0]):
        sums_ref[at] = sums[at * CO_DEV : (at + 1) * CO_DEV, :]


def fine_kernel(
    even_ref, nodes_ref, odd_ref, w_ends_ref, w_out_ref,
    edges_hbm, w_in_hbm, send_hbm, recv_hbm, wn_in_hbm, wn_out_hbm, after,
    new_hbm, out_ref, agg_ref, npart_ref, wn_agg_ref, wn_out_ref,
    edges_ref, w_self_ref, send_ref, recv_ref, wn_self_ref, new_ref, sems, out_sems,
):
    nodes = nodes_ref[...]
    count, width = nodes.shape
    copies = start_copies(
        [
            send_hbm, recv_hbm, edges_hbm, w_in_hbm.at[pl.ds(0, width)],
            wn_in_hbm.at[pl.ds(0, width)], wn_in_hbm.at[pl.ds(width, width)], wn_out_hbm,
        ],
        [send_ref, recv_ref, edges_ref, w_self_ref, wn_self_ref, wn_agg_ref, wn_out_ref],
        sems,
    )
    odd = (lax.axis_index(GROUP_AXES) % 2).astype(F32)
    met, other = even_ref[...].astype(F32), odd_ref[...].astype(F32)
    prev = (met * odd + other * (1.0 - odd)).astype(BF16)
    following = (other * odd + met * (1.0 - odd)).astype(BF16)
    extended = jnp.concatenate([prev, nodes, following], axis=0)
    ones = jnp.ones((count, 128), BF16)
    total = jnp.zeros((count, width), F32)
    for copy in copies[:4]:
        copy.wait()
    outs = []
    for at in range(0, edges_ref.shape[0], STEP):
        rows = pl.ds(at, STEP)
        picks = onehot_t(count, recv_ref[:, rows])
        senders = dot_t(onehot_t(extended.shape[0], send_ref[:, rows]), extended).astype(BF16)
        receivers = dot_t(picks, nodes).astype(BF16)
        valid = dot_t(picks, ones)[:, 0:1]
        edges = edges_ref[rows, :]
        pre = dot(edges, w_self_ref[...]) + dot(senders, w_ends_ref[0:width, :]) + dot(receivers, w_ends_ref[width:, :])
        hidden = silu(pre).astype(BF16)
        centred, scale = norm_parts(dot(hidden, w_out_ref[...]))
        new = (edges.astype(F32) + centred * (scale * valid)).astype(BF16)
        new_ref[rows, :] = new
        copy = pltpu.make_async_copy(new_ref.at[rows], new_hbm.at[rows], out_sems.at[at // STEP])
        copy.start()
        outs.append(copy)
        total = total + dot(picks, new)
    agg_ref[...] = total[0:TOP]
    for copy in copies[4:]:
        copy.wait()
    pre = dot(nodes, wn_self_ref[...])
    npart_ref[...] = pre[0:TOP]
    pre = pre + dot(total.astype(BF16), wn_agg_ref[...])
    hidden = silu(pre).astype(BF16)
    centred, scale = norm_parts(dot(hidden, wn_out_ref[...]))
    out_ref[...] = (nodes.astype(F32) + centred * scale).astype(BF16)
    for copy in outs:
        copy.wait()


def top_kernel(got_ref, agg_ref, part_ref, nodes_ref, wn_agg_ref, wn_out_ref, rest_ref, out_ref):
    width = agg_ref.shape[1]
    terms = [got_ref[at].astype(F32) for at in range(got_ref.shape[0])]
    while len(terms) > 1:
        half = len(terms) // 2
        terms = [a + b for a, b in zip(terms[:half], terms[half:])] + terms[2 * half :]
    sums = jnp.concatenate([terms[0], jnp.zeros((TOP - CO_DEV, width), F32)], axis=0)
    agg = (agg_ref[...] + sums).astype(BF16)
    hidden = silu(part_ref[...] + dot(agg, wn_agg_ref[...])).astype(BF16)
    centred, scale = norm_parts(dot(hidden, wn_out_ref[...]))
    out_ref[...] = (nodes_ref[0:TOP, :].astype(F32) + centred * scale).astype(BF16)


def in_hbm(*arrays):
    return [pltpu.with_memory_space_constraint(a, pltpu.HBM) for a in arrays]


def cost(flops, moved=0):
    return pl.CostEstimate(flops=flops, bytes_accessed=moved, transcendentals=0)


def call(kernel, name, outs, ins, out_specs=None, scratch=(), hbm=(), flops=0, **more):
    return pl.pallas_call(
        kernel,
        out_shape=outs,
        in_specs=[ANY if i in hbm else VMEM for i in range(len(ins))],
        out_specs=[VMEM] * len(outs) if out_specs is None else out_specs,
        scratch_shapes=scratch,
        compiler_params=pltpu.CompilerParams(vmem_limit_bytes=16 * MIB),
        cost_estimate=cost(flops),
        name=name,
        **more,
    )(*ins)


def body(
    node_latents,
    edge_latents,
    coarse_edges,
    w_edge_in,
    w_edge_out,
    w_node_in,
    w_node_out,
    fine_senders,
    fine_receivers,
    halo_lists,
    coarse_senders,
    coarse_receivers,
):
    count, width = node_latents.shape
    edge_count = edge_latents.shape[0]
    cedge_count = coarse_edges.shape[0]
    halo = halo_lists.shape[2]
    group = lax.axis_size(GROUP_AXES)
    coarse_count = group * CO_DEV
    shape = jax.ShapeDtypeStruct
    like = lambda a: shape(a.shape, a.dtype)
    vmem = pltpu.VMEM
    dma = pltpu.SemaphoreType.DMA
    square = 2 * width * width
    blocks = shape((group, CO_DEV, width), BF16)
    ids = lambda a: a[None, :]

    (head,) = call(
        head_kernel, "head", (shape((CO_DEV, width), BF16),), in_hbm(node_latents), hbm=(0,),
        scratch=[vmem((TOP, width), BF16), dma(())],
    )
    sub, patch = lax.axis_size("sub"), lax.axis_size("patch")
    assert sub & (sub - 1) == 0 and patch % 2 == 0
    masks = list(reversed(range(1, sub)))
    turns = sorted(range(1, patch), key=lambda by: (min(by, patch - by), by))
    near = [swap(head, mask, "sub") for mask in masks]
    nodes, cedges, w_ends, w_out, to_even, to_odd, gather, picks, coarse_part = call(
        load_kernel,
        "load",
        (
            like(node_latents),
            like(coarse_edges),
            shape((2 * width, width), BF16),
            like(w_edge_out),
            shape((halo, width), BF16),
            shape((halo, width), BF16),
            shape((2 * cedge_count, coarse_count), BF16),
            shape((coarse_count, cedge_count), BF16),
            shape((cedge_count, width), F32),
        ),
        in_hbm(node_latents, halo_lists, coarse_edges, w_edge_in, ids(coarse_senders), ids(coarse_receivers), w_edge_out)
        + [head],
        hbm=range(8),
        scratch=[
            vmem(halo_lists.shape, jnp.int32), vmem((width, width), BF16),
            vmem((1, cedge_count), jnp.int32), vmem((1, cedge_count), jnp.int32), dma((8,)),
        ],
        flops=edge_count * square,
    )
    (lat,) = call(
        functools.partial(join_kernel, masks), "join", (shape((sub * CO_DEV, width), BF16),), [head] + near + [nodes], hbm=(sub,),
    )
    far = [turn(lat, by) for by in turns]
    to_even, to_odd = call(
        pass_kernel, "pass", (like(to_even), like(to_odd)), [to_even, to_odd, lat], hbm=range(3), out_specs=[ANY, ANY],
        input_output_aliases={0: 0, 1: 1},
    )
    from_even, from_odd = pair(to_even, 0), pair(to_odd, 1)
    new_coarse, sums = call(
        functools.partial(coarse_kernel, turns), "coarse", (like(coarse_edges), blocks),
        [lat] + far + [cedges, coarse_part, gather, picks, w_ends, w_out], flops=0,
    )
    got = lax.all_to_all(sums, GROUP_AXES, 0, 0)
    new_edges, rest, agg, node_part, wn_agg, wn_out = call(
        fine_kernel,
        "fine",
        (
            like(edge_latents),
            like(node_latents),
            shape((TOP, width), F32),
            shape((TOP, width), F32),
            shape((width, width), BF16),
            like(w_node_out),
        ),
        [from_even, nodes, from_odd, w_ends, w_out]
        + in_hbm(edge_latents, w_edge_in, ids(fine_senders), ids(fine_receivers), w_node_in, w_node_out)
        + [sums],
        hbm=range(5, 12),
        out_specs=[ANY] + [VMEM] * 5,
        scratch=[
            vmem(edge_latents.shape, BF16), vmem((width, width), BF16), vmem((1, edge_count), jnp.int32),
            vmem((1, edge_count), jnp.int32), vmem((width, width), BF16), vmem(edge_latents.shape, BF16), dma((7,)),
            dma((edge_count // STEP,)),
        ],
        flops=64 * edge_count * square,
    )
    new_nodes = pl.pallas_call(
        top_kernel,
        grid=(1,),
        out_shape=like(node_latents),
        in_specs=[VMEM] * 6 + [ANY],
        out_specs=pl.BlockSpec((TOP, width), lambda i: (0, 0)),
        input_output_aliases={6: 0},
        compiler_params=pltpu.CompilerParams(vmem_limit_bytes=16 * MIB),
        name="top",
    )(got, agg, node_part, nodes, wn_agg, wn_out, rest)
    return (new_nodes, new_edges, new_coarse)


def solution(mesh):
    rows = P(("parts", "patch", "sub"), None)
    ids = P(("parts", "patch", "sub"))
    in_specs = (
        rows, rows, rows, P(), P(), P(), P(), ids, ids, P(("parts", "patch", "sub"), None, None), ids, ids,
    )
    return jax.shard_map(body, mesh=mesh, in_specs=in_specs, out_specs=(rows, rows, rows), check_vma=False)
```

profile of v0, /device:TPU:0, one launch (start us, length us, event | category | flops | bytes accessed | tf_op | source)
XLA Modules:
  0.0 28.7 jit_solution(11029072511490079915)
XLA Ops:
  0.6 0.7 %head.1.after.refs_0_ = bf16[4,512]{1,0:T(4,128)(2,1)S(1)} custom-call(bf16[128,512]{1,0:T(8,128)(2,1)} %nodes_hbm.3), custom_call_target="tpu_custom_call" | custom-call | tf_op jit(solution)/shard_map/head/pallas_call | solution.py:239
  1.4 2.4 %collective-permute-start = (bf16[4,512]{1,0:T(4,128)(2,1)S(1)}, bf16[4,512]{1,0:T(4,128)(2,1)S(1)}, u32[]{:S(2)}, u32[]{:S(2)}) collective-permute-start(bf16[4,512]{1,0:T(4,128)(2,1)S(1)} %head.1.after.refs_0_), channel_id=1, source_target_pairs={{0,3},{1,2},{2,1},{3,0},{4,7},{5,6},{6,5},{7,4},{8,11},{9,10},{10,... | collective-permute-start | bytes 12296 | tf_op jit(solution)/shard_map/ppermute | solution.py:21
  3.8 0.6 %collective-permute-start.1 = (bf16[4,512]{1,0:T(4,128)(2,1)S(1)}, bf16[4,512]{1,0:T(4,128)(2,1)S(1)}, u32[]{:S(2)}, u32[]{:S(2)}) collective-permute-start(bf16[4,512]{1,0:T(4,128)(2,1)S(1)} %head.1.after.refs_0_), channel_id=1, source_target_pairs={{0,2},{1,3},{2,0},{3,1},{4,6},{5,7},{6,4},{7,5},{8,10},{9,11},{10,... | collective-permute-start | bytes 12296 | tf_op jit(solution)/shard_map/ppermute | solution.py:21
  4.5 0.0 collective-permute-start.2
  4.5 1.7 %load.1 = (bf16[128,512]{1,0:T(8,128)(2,1)S(1)}, bf16[64,512]{1,0:T(8,128)(2,1)S(1)}, bf16[1024,512]{1,0:T(8,128)(2,1)S(1)}, bf16[512,512]{1,0:T(8,128)(2,1)S(1)...) custom-call(bf16[128,512]{1,0:T(8,128)(2,1)} %nodes_hbm.3, ...), custom_call_target="tpu_custom_call" | custom-call | flops 268435456 | tf_op jit(solution)/shard_map/load/pallas_call | solution.py:239
  6.2 0.0 collective-permute-done.refs_1_
  6.2 1.2 %collective-permute-done.1.refs_2_ = bf16[4,512]{1,0:T(4,128)(2,1)S(1)} collective-permute-done((bf16[4,512]{1,0:T(4,128)(2,1)S(1)}, bf16[4,512]{1,0:T(4,128)(2,1)S(1)}, u32[]{:S(2)}, u32[]{:S(2)}) %collective-permute-start.1) | collective-permute-done | bytes 4128 | tf_op jit(solution)/shard_map/ppermute | solution.py:21
  7.4 0.0 collective-permute-done.2.refs_3_
  7.4 2.6 %collective-permute-start.3 = (bf16[16,512]{1,0:T(8,128)(2,1)S(1)}, bf16[16,512]{1,0:T(8,128)(2,1)S(1)}, u32[]{:S(2)}, u32[]{:S(2)}) collective-permute-start(bf16[16,512]{1,0:T(8,128)(2,1)S(1)} %join.1.refs_0_.after), channel_id=1, source_target_pairs={{0,8},{8,4},{4,12},{12,0},{1,9},{9,5},{5,13},{13,1},{2,10},{10,6},... | collective-permute-start | bytes 49160 | tf_op jit(solution)/shard_map/ppermute | solution.py:36
  10.1 1.2 %collective-permute-start.4 = (bf16[16,512]{1,0:T(8,128)(2,1)S(1)}, bf16[16,512]{1,0:T(8,128)(2,1)S(1)}, u32[]{:S(2)}, u32[]{:S(2)}) collective-permute-start(bf16[16,512]{1,0:T(8,128)(2,1)S(1)} %join.1.refs_0_.after), channel_id=1, source_target_pairs={{0,12},{8,0},{4,8},{12,4},{1,13},{9,1},{5,9},{13,5},{2,14},{10,2},... | collective-permute-start | bytes 49160 | tf_op jit(solution)/shard_map/ppermute | solution.py:36
  11.3 0.3 %collective-permute-start.5 = (bf16[16,512]{1,0:T(8,128)(2,1)S(1)}, bf16[16,512]{1,0:T(8,128)(2,1)S(1)}, u32[]{:S(2)}, u32[]{:S(2)}) collective-permute-start(bf16[16,512]{1,0:T(8,128)(2,1)S(1)} %join.1.refs_0_.after), channel_id=1, source_target_pairs={{0,4},{8,12},{4,0},{12,8},{1,5},{9,13},{5,1},{13,9},{2,6},{10,14},... | collective-permute-start | bytes 49160 | tf_op jit(solution)/shard_map/ppermute | solution.py:36
  11.7 0.0 collective-permute-start.6
  11.7 3.0 %collective-permute-start.7 = (bf16[16,512]{1,0:T(8,128)(2,1)S(1)}, bf16[16,512]{1,0:T(8,128)(2,1)S(1)}, u32[]{:S(2)}, u32[]{:S(2)}) collective-permute-start(bf16[16,512]{1,0:T(8,128)(2,1)S(1)} %get-tuple-element.33), channel_id=1, source_target_pairs={{1,2},{3,4},{5,6},{7,8},{9,10},{11,12},{13,14},{15,0},{2,1},{4,3},... | collective-permute-start | bytes 49160 | tf_op jit(solution)/shard_map/ppermute | solution.py:42
  14.7 0.0 collective-permute-done.3.refs_1_
  14.7 0.1 collective-permute-done.4.refs_2_
  14.7 0.3 %collective-permute-done.5.refs_3_ = bf16[16,512]{1,0:T(8,128)(2,1)S(1)} collective-permute-done((bf16[16,512]{1,0:T(8,128)(2,1)S(1)}, bf16[16,512]{1,0:T(8,128)(2,1)S(1)}, u32[]{:S(2)}, u32[]{:S(2)}) %collective-permute-start.5) | collective-permute-done | bytes 16416 | tf_op jit(solution)/shard_map/ppermute | solution.py:36
  15.0 1.5 %coarse.1 = (bf16[64,512]{1,0:T(8,128)(2,1)}, bf16[16,4,512]{2,1,0:T(4,128)(2,1)}) custom-call(bf16[16,512]{1,0:T(8,128)(2,1)S(1)} %join.1.refs_0_.after, bf16[16,512]{1,0:T(8,128)(2,1)S(1)} %collective-permute-done.3.refs_1_, bf16[16,512]{1,0:T(8,128)(2,1)S(1)} %collective-permute-done.4.refs_2_, bf16[16,512]{1,0:T(8,128)(2,1)S(1)} %collective-permute-done.5.refs_3_, ...), custom_call_target="tpu_custom_call" | custom-call | tf_op jit(solution)/shard_map/coarse/pallas_call | solution.py:239
  16.6 4.2 %all-to-all-start = ((bf16[16,4,512]{2,1,0:T(4,128)(2,1)}), bf16[16,4,512]{2,1,0:T(4,128)(2,1)S(1)}, u32[]{:S(2)}, u32[]{:S(2)}) async-start(bf16[16,4,512]{2,1,0:T(4,128)(2,1)} %get-tuple-element.29.after), calls=%async_computation | async-start | bytes 131072 | tf_op jit(solution)/shard_map/all_to_all | solution.py:325
  20.7 0.0 collective-permute-done.6.even_ref
  20.7 0.0 collective-permute-done.7.odd_ref
  20.7 6.4 %fine.1 = (bf16[512,512]{1,0:T(8,128)(2,1)}, bf16[128,512]{1,0:T(8,128)(2,1)}, f32[16,512]{1,0:T(8,128)S(1)}, f32[16,512]{1,0:T(8,128)S(1)}, bf16[512,512]{1,0:T(8,128)(2,1)S(1)}, /*index=5*/bf16[512,512]{1,0:T(8,128)(2,1)S(1)}) custom-call(bf16[16,512]{1,0:T(8,128)(2,1)S(1)} %collective-permute-done.6.even_ref, ...), custom_call_target="tpu_custom_call" | custom-call | flops 17179869184 | tf_op jit(solution)/shard_map/fine/pallas_call | solution.py:239
  27.1 0.5 %all-to-all-done.got_ref = bf16[16,4,512]{2,1,0:T(4,128)(2,1)S(1)} async-done(((bf16[16,4,512]{2,1,0:T(4,128)(2,1)}), bf16[16,4,512]{2,1,0:T(4,128)(2,1)S(1)}, u32[]{:S(2)}, u32[]{:S(2)}) %all-to-all-start) | async-done | bytes 65568 | tf_op jit(solution)/shard_map/all_to_all | solution.py:325
  27.6 1.1 %top.1 = bf16[128,512]{1,0:T(8,128)(2,1)} custom-call(bf16[16,4,512]{2,1,0:T(4,128)(2,1)S(1)} %all-to-all-done.got_ref, f32[16,512]{1,0:T(8,128)S(1)} %get-tuple-element.34.agg_ref, f32[16,512]{1,0:T(8,128)S(1)} %get-tuple-element.35.part_ref, bf16[128,512]{1,0:T(8,128)(2,1)S(1)} %get-tuple-element.22.refs_4_.nodes_ref, ...), custom_call_target="tpu_custom_call", output_to_operand_aliasing={{}: (6, {})} | custom-call | tf_op jit(solution)/shard_map/top/pallas_call | solution.py:349
  (2 shorter events, 0.0 us)
Async XLA Ops:
  1.4 4.9 %collective-permute-start = (bf16[4,512]{1,0:T(4,128)(2,1)S(1)}, bf16[4,512]{1,0:T(4,128)(2,1)S(1)}, u32[]{:S(2)}, u32[]{:S(2)}) collective-permute-start(bf16[4,512]{1,0:T(4,128)(2,1)S(1)} %head.1.after.refs_0_), channel_id=1, source_target_pairs={{0,3},{1,2},{2,1},{3,0},{4,7},{5,6},{6,5},{7,4},{8,11},{9,10},{10,... | collective-permute-start | bytes 12296 | tf_op jit(solution)/shard_map/ppermute | solution.py:21
  3.8 3.6 %collective-permute-start.1 = (bf16[4,512]{1,0:T(4,128)(2,1)S(1)}, bf16[4,512]{1,0:T(4,128)(2,1)S(1)}, u32[]{:S(2)}, u32[]{:S(2)}) collective-permute-start(bf16[4,512]{1,0:T(4,128)(2,1)S(1)} %head.1.after.refs_0_), channel_id=1, source_target_pairs={{0,2},{1,3},{2,0},{3,1},{4,6},{5,7},{6,4},{7,5},{8,10},{9,11},{10,... | collective-permute-start | bytes 12296 | tf_op jit(solution)/shard_map/ppermute | solution.py:21
  4.5 3.0 %collective-permute-start.2 = (bf16[4,512]{1,0:T(4,128)(2,1)S(1)}, bf16[4,512]{1,0:T(4,128)(2,1)S(1)}, u32[]{:S(2)}, u32[]{:S(2)}) collective-permute-start(bf16[4,512]{1,0:T(4,128)(2,1)S(1)} %head.1.after.refs_0_), channel_id=1, source_target_pairs={{0,1},{1,0},{2,3},{3,2},{4,5},{5,4},{6,7},{7,6},{8,9},{9,8},{10,11... | collective-permute-start | bytes 12296 | tf_op jit(solution)/shard_map/ppermute | solution.py:21
  7.4 7.2 %collective-permute-start.3 = (bf16[16,512]{1,0:T(8,128)(2,1)S(1)}, bf16[16,512]{1,0:T(8,128)(2,1)S(1)}, u32[]{:S(2)}, u32[]{:S(2)}) collective-permute-start(bf16[16,512]{1,0:T(8,128)(2,1)S(1)} %join.1.refs_0_.after), channel_id=1, source_target_pairs={{0,8},{8,4},{4,12},{12,0},{1,9},{9,5},{5,13},{13,1},{2,10},{10,6},... | collective-permute-start | bytes 49160 | tf_op jit(solution)/shard_map/ppermute | solution.py:36
  10.1 4.6 %collective-permute-start.4 = (bf16[16,512]{1,0:T(8,128)(2,1)S(1)}, bf16[16,512]{1,0:T(8,128)(2,1)S(1)}, u32[]{:S(2)}, u32[]{:S(2)}) collective-permute-start(bf16[16,512]{1,0:T(8,128)(2,1)S(1)} %join.1.refs_0_.after), channel_id=1, source_target_pairs={{0,12},{8,0},{4,8},{12,4},{1,13},{9,1},{5,9},{13,5},{2,14},{10,2},... | collective-permute-start | bytes 49160 | tf_op jit(solution)/shard_map/ppermute | solution.py:36
  11.3 3.7 %collective-permute-start.5 = (bf16[16,512]{1,0:T(8,128)(2,1)S(1)}, bf16[16,512]{1,0:T(8,128)(2,1)S(1)}, u32[]{:S(2)}, u32[]{:S(2)}) collective-permute-start(bf16[16,512]{1,0:T(8,128)(2,1)S(1)} %join.1.refs_0_.after), channel_id=1, source_target_pairs={{0,4},{8,12},{4,0},{12,8},{1,5},{9,13},{5,1},{13,9},{2,6},{10,14},... | collective-permute-start | bytes 49160 | tf_op jit(solution)/shard_map/ppermute | solution.py:36
  11.7 9.1 %collective-permute-start.6 = (bf16[16,512]{1,0:T(8,128)(2,1)S(1)}, bf16[16,512]{1,0:T(8,128)(2,1)S(1)}, u32[]{:S(2)}, u32[]{:S(2)}) collective-permute-start(bf16[16,512]{1,0:T(8,128)(2,1)S(1)} %get-tuple-element.32), channel_id=1, source_target_pairs={{0,1},{2,3},{4,5},{6,7},{8,9},{10,11},{12,13},{14,15},{1,0},{3,2},... | collective-permute-start | bytes 49160 | tf_op jit(solution)/shard_map/ppermute | solution.py:42
  11.7 9.1 %collective-permute-start.7 = (bf16[16,512]{1,0:T(8,128)(2,1)S(1)}, bf16[16,512]{1,0:T(8,128)(2,1)S(1)}, u32[]{:S(2)}, u32[]{:S(2)}) collective-permute-start(bf16[16,512]{1,0:T(8,128)(2,1)S(1)} %get-tuple-element.33), channel_id=1, source_target_pairs={{1,2},{3,4},{5,6},{7,8},{9,10},{11,12},{13,14},{15,0},{2,1},{4,3},... | collective-permute-start | bytes 49160 | tf_op jit(solution)/shard_map/ppermute | solution.py:42
  16.6 11.1 %all-to-all-start = ((bf16[16,4,512]{2,1,0:T(4,128)(2,1)}), bf16[16,4,512]{2,1,0:T(4,128)(2,1)S(1)}, u32[]{:S(2)}, u32[]{:S(2)}) async-start(bf16[16,4,512]{2,1,0:T(4,128)(2,1)} %get-tuple-element.29.after), calls=%async_computation | async-start | bytes 131072 | tf_op jit(solution)/shard_map/all_to_all | solution.py:325
where the time goes:
time: 29.1 us; the launch traced here: 28.7 us
  starting transfers between devices  14.5 us (50%)
  Pallas kernels  11.5 us (40%)
  waiting for transfers between devices  2.07 us (7%)
  between operations  0.7 us (2%)
    pallas_call x6, Pallas kernels, call(): pl.pallas_call(kernel, out_shape=outs, in_specs=[ANY if i in hbm else VME...  10.4 us
    ppermute x3, starting transfers between devices, turn(): lax.ppermute(value, 'patch', [(ring[i], ring[(i + by) % devices]) for i i...  4.22 us
    all_to_all x1, starting transfers between devices, body(): got = lax.all_to_all(sums, GROUP_AXES, 0, 0)  4.16 us
    ppermute x3, starting transfers between devices, swap(): lax.ppermute(value, axis, [(i, i ^ mask) for i in range(lax.axis_size(axi...  3.12 us
    ppermute x2, starting transfers between devices, pair(): return lax.ppermute(value, GROUP_AXES, pairs + [(b, a) for a, b in pairs])  3 us
    ppermute x3, waiting for transfers between devices, swap(): lax.ppermute(value, axis, [(i, i ^ mask) for i in range(lax.axis_size(axi...  1.18 us
    pallas_call x1, Pallas kernels, body(): pl.pallas_call(top_kernel, grid=(1,), out_shape=like(node_latents), in_sp...  1.12 us
  transfers between devices with their start and end apart: 9, of which 4 were waited for; matrix products, arithmetic and copies ran while one was open for 0% of the time, Pallas kernels for 34%

commit v1 on v0

--- a/solution.py
+++ b/solution.py
@@ -10,7 +10,7 @@
 CO_DEV = 4
 GROUP_AXES = ("patch", "sub")
 TOP = 16
-STEP = 128
+STEP = 256
 MIB = 1 << 20
 ANY = pl.BlockSpec(memory_space=pl.ANY)
 VMEM = pl.BlockSpec(memory_space=pltpu.VMEM)
@@ -182,7 +182,7 @@
     extended = jnp.concatenate([prev, nodes, following], axis=0)
     ones = jnp.ones((count, 128), BF16)
     total = jnp.zeros((count, width), F32)
-    for copy in copies[:4]:
+    for copy in copies[:2]:
         copy.wait()
     outs = []
     for at in range(0, edges_ref.shape[0], STEP):
@@ -191,8 +191,12 @@
         senders = dot_t(onehot_t(extended.shape[0], send_ref[:, rows]), extended).astype(BF16)
         receivers = dot_t(picks, nodes).astype(BF16)
         valid = dot_t(picks, ones)[:, 0:1]
+        pre = dot(jnp.concatenate([senders, receivers], axis=1), w_ends_ref[...])
+        if at == 0:
+            for copy in copies[2:4]:
+                copy.wait()
         edges = edges_ref[rows, :]
-        pre = dot(edges, w_self_ref[...]) + dot(senders, w_ends_ref[0:width, :]) + dot(receivers, w_ends_ref[width:, :])
+        pre = pre + dot(edges, w_self_ref[...])
         hidden = silu(pre).astype(BF16)
         centred, scale = norm_parts(dot(hidden, w_out_ref[...]))
         new = (edges.astype(F32) + centred * (scale * valid)).astype(BF16)

time: 29.1 us -> 29.1 us (level)
  Pallas kernels: 11.5 us -> 9.86 us
  waiting for transfers between devices: 2.07 us -> 3.69 us
    pallas_call x6, Pallas kernels: 10.4 us -> 8.74 us  [call(): pl.pallas_call(kernel, out_shape=outs, in_specs=[ANY if i in hbm else VME...]
    all_to_all x1, waiting for transfers between devices: 0.49 us -> 2.11 us  [body(): got = lax.all_to_all(sums, GROUP_AXES, 0, 0)]
  transfers between devices with their start and end apart: 9 -> 9, of which waited for: 4 -> 4; matrix products, arithmetic and copies ran while one was open for 0% -> 0% of each run, Pallas kernels for 34% -> 28%
where the time goes in v1:
time: 29.1 us; the launch traced here: 28.7 us
  starting transfers between devices  14.5 us (50%)
  Pallas kernels  9.86 us (34%)
  waiting for transfers between devices  3.69 us (13%)
  between operations  0.7 us (2%)
    pallas_call x6, Pallas kernels, call(): pl.pallas_call(kernel, out_shape=outs, in_specs=[ANY if i in hbm else VME...  8.74 us
    ppermute x3, starting transfers between devices, turn(): lax.ppermute(value, 'patch', [(ring[i], ring[(i + by) % devices]) for i i...  4.22 us
    all_to_all x1, starting transfers between devices, body(): got = lax.all_to_all(sums, GROUP_AXES, 0, 0)  4.16 us
    ppermute x3, starting transfers between devices, swap(): lax.ppermute(value, axis, [(i, i ^ mask) for i in range(lax.axis_size(axi...  3.12 us
    ppermute x2, starting transfers between devices, pair(): return lax.ppermute(value, GROUP_AXES, pairs + [(b, a) for a, b in pairs])  3 us
    all_to_all x1, waiting for transfers between devices, body(): got = lax.all_to_all(sums, GROUP_AXES, 0, 0)  2.11 us
    ppermute x3, waiting for transfers between devices, swap(): lax.ppermute(value, axis, [(i, i ^ mask) for i in range(lax.axis_size(axi...  1.18 us
    pallas_call x1, Pallas kernels, body(): pl.pallas_call(top_kernel, grid=(1,), out_shape=like(node_latents), in_sp...  1.12 us
  transfers between devices with their start and end apart: 9, of which 4 were waited for; matrix products, arithmetic and copies ran while one was open for 0% of the time, Pallas kernels for 28%

profile of v1, /device:TPU:0, one launch (start us, length us, event | category | flops | bytes accessed | tf_op | source)
XLA Modules:
  0.0 28.7 jit_solution(9937399991150485463)
XLA Ops:
  0.6 0.7 %head.1.after.refs_0_ = bf16[4,512]{1,0:T(4,128)(2,1)S(1)} custom-call(bf16[128,512]{1,0:T(8,128)(2,1)} %nodes_hbm.3), custom_call_target="tpu_custom_call" | custom-call | tf_op jit(solution)/shard_map/head/pallas_call | solution.py:243
  1.4 2.4 %collective-permute-start = (bf16[4,512]{1,0:T(4,128)(2,1)S(1)}, bf16[4,512]{1,0:T(4,128)(2,1)S(1)}, u32[]{:S(2)}, u32[]{:S(2)}) collective-permute-start(bf16[4,512]{1,0:T(4,128)(2,1)S(1)} %head.1.after.refs_0_), channel_id=1, source_target_pairs={{0,3},{1,2},{2,1},{3,0},{4,7},{5,6},{6,5},{7,4},{8,11},{9,10},{10,... | collective-permute-start | bytes 12296 | tf_op jit(solution)/shard_map/ppermute | solution.py:21
  3.8 0.6 %collective-permute-start.1 = (bf16[4,512]{1,0:T(4,128)(2,1)S(1)}, bf16[4,512]{1,0:T(4,128)(2,1)S(1)}, u32[]{:S(2)}, u32[]{:S(2)}) collective-permute-start(bf16[4,512]{1,0:T(4,128)(2,1)S(1)} %head.1.after.refs_0_), channel_id=1, source_target_pairs={{0,2},{1,3},{2,0},{3,1},{4,6},{5,7},{6,4},{7,5},{8,10},{9,11},{10,... | collective-permute-start | bytes 12296 | tf_op jit(solution)/shard_map/ppermute | solution.py:21
  4.5 0.0 collective-permute-start.2
  4.5 1.7 %load.1 = (bf16[128,512]{1,0:T(8,128)(2,1)S(1)}, bf16[64,512]{1,0:T(8,128)(2,1)S(1)}, bf16[1024,512]{1,0:T(8,128)(2,1)S(1)}, bf16[512,512]{1,0:T(8,128)(2,1)S(1)...) custom-call(bf16[128,512]{1,0:T(8,128)(2,1)} %nodes_hbm.3, ...), custom_call_target="tpu_custom_call" | custom-call | flops 268435456 | tf_op jit(solution)/shard_map/load/pallas_call | solution.py:243
  6.2 0.0 collective-permute-done.refs_1_
  6.2 1.2 %collective-permute-done.1.refs_2_ = bf16[4,512]{1,0:T(4,128)(2,1)S(1)} collective-permute-done((bf16[4,512]{1,0:T(4,128)(2,1)S(1)}, bf16[4,512]{1,0:T(4,128)(2,1)S(1)}, u32[]{:S(2)}, u32[]{:S(2)}) %collective-permute-start.1) | collective-permute-done | bytes 4128 | tf_op jit(solution)/shard_map/ppermute | solution.py:21
  7.4 0.0 collective-permute-done.2.refs_3_
  7.4 2.6 %collective-permute-start.3 = (bf16[16,512]{1,0:T(8,128)(2,1)S(1)}, bf16[16,512]{1,0:T(8,128)(2,1)S(1)}, u32[]{:S(2)}, u32[]{:S(2)}) collective-permute-start(bf16[16,512]{1,0:T(8,128)(2,1)S(1)} %join.1.refs_0_.after), channel_id=1, source_target_pairs={{0,8},{8,4},{4,12},{12,0},{1,9},{9,5},{5,13},{13,1},{2,10},{10,6},... | collective-permute-start | bytes 49160 | tf_op jit(solution)/shard_map/ppermute | solution.py:36
  10.1 1.2 %collective-permute-start.4 = (bf16[16,512]{1,0:T(8,128)(2,1)S(1)}, bf16[16,512]{1,0:T(8,128)(2,1)S(1)}, u32[]{:S(2)}, u32[]{:S(2)}) collective-permute-start(bf16[16,512]{1,0:T(8,128)(2,1)S(1)} %join.1.refs_0_.after), channel_id=1, source_target_pairs={{0,12},{8,0},{4,8},{12,4},{1,13},{9,1},{5,9},{13,5},{2,14},{10,2},... | collective-permute-start | bytes 49160 | tf_op jit(solution)/shard_map/ppermute | solution.py:36
  11.3 0.3 %collective-permute-start.5 = (bf16[16,512]{1,0:T(8,128)(2,1)S(1)}, bf16[16,512]{1,0:T(8,128)(2,1)S(1)}, u32[]{:S(2)}, u32[]{:S(2)}) collective-permute-start(bf16[16,512]{1,0:T(8,128)(2,1)S(1)} %join.1.refs_0_.after), channel_id=1, source_target_pairs={{0,4},{8,12},{4,0},{12,8},{1,5},{9,13},{5,1},{13,9},{2,6},{10,14},... | collective-permute-start | bytes 49160 | tf_op jit(solution)/shard_map/ppermute | solution.py:36
  11.7 0.0 collective-permute-start.6
  11.7 3.0 %collective-permute-start.7 = (bf16[16,512]{1,0:T(8,128)(2,1)S(1)}, bf16[16,512]{1,0:T(8,128)(2,1)S(1)}, u32[]{:S(2)}, u32[]{:S(2)}) collective-permute-start(bf16[16,512]{1,0:T(8,128)(2,1)S(1)} %get-tuple-element.33), channel_id=1, source_target_pairs={{1,2},{3,4},{5,6},{7,8},{9,10},{11,12},{13,14},{15,0},{2,1},{4,3},... | collective-permute-start | bytes 49160 | tf_op jit(solution)/shard_map/ppermute | solution.py:42
  14.7 0.0 collective-permute-done.3.refs_1_
  14.7 0.1 collective-permute-done.4.refs_2_
  14.7 0.3 %collective-permute-done.5.refs_3_ = bf16[16,512]{1,0:T(8,128)(2,1)S(1)} collective-permute-done((bf16[16,512]{1,0:T(8,128)(2,1)S(1)}, bf16[16,512]{1,0:T(8,128)(2,1)S(1)}, u32[]{:S(2)}, u32[]{:S(2)}) %collective-permute-start.5) | collective-permute-done | bytes 16416 | tf_op jit(solution)/shard_map/ppermute | solution.py:36
  15.0 1.5 %coarse.1 = (bf16[64,512]{1,0:T(8,128)(2,1)}, bf16[16,4,512]{2,1,0:T(4,128)(2,1)}) custom-call(bf16[16,512]{1,0:T(8,128)(2,1)S(1)} %join.1.refs_0_.after, bf16[16,512]{1,0:T(8,128)(2,1)S(1)} %collective-permute-done.3.refs_1_, bf16[16,512]{1,0:T(8,128)(2,1)S(1)} %collective-permute-done.4.refs_2_, bf16[16,512]{1,0:T(8,128)(2,1)S(1)} %collective-permute-done.5.refs_3_, ...), custom_call_target="tpu_custom_call" | custom-call | tf_op jit(solution)/shard_map/coarse/pallas_call | solution.py:243
  16.6 4.2 %all-to-all-start = ((bf16[16,4,512]{2,1,0:T(4,128)(2,1)}), bf16[16,4,512]{2,1,0:T(4,128)(2,1)S(1)}, u32[]{:S(2)}, u32[]{:S(2)}) async-start(bf16[16,4,512]{2,1,0:T(4,128)(2,1)} %get-tuple-element.29.after), calls=%async_computation | async-start | bytes 131072 | tf_op jit(solution)/shard_map/all_to_all | solution.py:329
  20.7 0.0 collective-permute-done.6.even_ref
  20.7 0.0 collective-permute-done.7.odd_ref
  20.7 4.8 %fine.1 = (bf16[512,512]{1,0:T(8,128)(2,1)}, bf16[128,512]{1,0:T(8,128)(2,1)}, f32[16,512]{1,0:T(8,128)S(1)}, f32[16,512]{1,0:T(8,128)S(1)}, bf16[512,512]{1,0:T(8,128)(2,1)S(1)}, /*index=5*/bf16[512,512]{1,0:T(8,128)(2,1)S(1)}) custom-call(bf16[16,512]{1,0:T(8,128)(2,1)S(1)} %collective-permute-done.6.even_ref, ...), custom_call_target="tpu_custom_call" | custom-call | flops 17179869184 | tf_op jit(solution)/shard_map/fine/pallas_call | solution.py:243
  25.5 2.1 %all-to-all-done.got_ref = bf16[16,4,512]{2,1,0:T(4,128)(2,1)S(1)} async-done(((bf16[16,4,512]{2,1,0:T(4,128)(2,1)}), bf16[16,4,512]{2,1,0:T(4,128)(2,1)S(1)}, u32[]{:S(2)}, u32[]{:S(2)}) %all-to-all-start) | async-done | bytes 65568 | tf_op jit(solution)/shard_map/all_to_all | solution.py:329
  27.6 1.1 %top.1 = bf16[128,512]{1,0:T(8,128)(2,1)} custom-call(bf16[16,4,512]{2,1,0:T(4,128)(2,1)S(1)} %all-to-all-done.got_ref, f32[16,512]{1,0:T(8,128)S(1)} %get-tuple-element.34.agg_ref, f32[16,512]{1,0:T(8,128)S(1)} %get-tuple-element.35.part_ref, bf16[128,512]{1,0:T(8,128)(2,1)S(1)} %get-tuple-element.22.refs_4_.nodes_ref, ...), custom_call_target="tpu_custom_call", output_to_operand_aliasing={{}: (6, {})} | custom-call | tf_op jit(solution)/shard_map/top/pallas_call | solution.py:353
  (2 shorter events, 0.0 us)
Async XLA Ops:
  1.4 4.9 %collective-permute-start = (bf16[4,512]{1,0:T(4,128)(2,1)S(1)}, bf16[4,512]{1,0:T(4,128)(2,1)S(1)}, u32[]{:S(2)}, u32[]{:S(2)}) collective-permute-start(bf16[4,512]{1,0:T(4,128)(2,1)S(1)} %head.1.after.refs_0_), channel_id=1, source_target_pairs={{0,3},{1,2},{2,1},{3,0},{4,7},{5,6},{6,5},{7,4},{8,11},{9,10},{10,... | collective-permute-start | bytes 12296 | tf_op jit(solution)/shard_map/ppermute | solution.py:21
  3.8 3.6 %collective-permute-start.1 = (bf16[4,512]{1,0:T(4,128)(2,1)S(1)}, bf16[4,512]{1,0:T(4,128)(2,1)S(1)}, u32[]{:S(2)}, u32[]{:S(2)}) collective-permute-start(bf16[4,512]{1,0:T(4,128)(2,1)S(1)} %head.1.after.refs_0_), channel_id=1, source_target_pairs={{0,2},{1,3},{2,0},{3,1},{4,6},{5,7},{6,4},{7,5},{8,10},{9,11},{10,... | collective-permute-start | bytes 12296 | tf_op jit(solution)/shard_map/ppermute | solution.py:21
  4.5 3.0 %collective-permute-start.2 = (bf16[4,512]{1,0:T(4,128)(2,1)S(1)}, bf16[4,512]{1,0:T(4,128)(2,1)S(1)}, u32[]{:S(2)}, u32[]{:S(2)}) collective-permute-start(bf16[4,512]{1,0:T(4,128)(2,1)S(1)} %head.1.after.refs_0_), channel_id=1, source_target_pairs={{0,1},{1,0},{2,3},{3,2},{4,5},{5,4},{6,7},{7,6},{8,9},{9,8},{10,11... | collective-permute-start | bytes 12296 | tf_op jit(solution)/shard_map/ppermute | solution.py:21
  7.4 7.2 %collective-permute-start.3 = (bf16[16,512]{1,0:T(8,128)(2,1)S(1)}, bf16[16,512]{1,0:T(8,128)(2,1)S(1)}, u32[]{:S(2)}, u32[]{:S(2)}) collective-permute-start(bf16[16,512]{1,0:T(8,128)(2,1)S(1)} %join.1.refs_0_.after), channel_id=1, source_target_pairs={{0,8},{8,4},{4,12},{12,0},{1,9},{9,5},{5,13},{13,1},{2,10},{10,6},... | collective-permute-start | bytes 49160 | tf_op jit(solution)/shard_map/ppermute | solution.py:36
  10.1 4.6 %collective-permute-start.4 = (bf16[16,512]{1,0:T(8,128)(2,1)S(1)}, bf16[16,512]{1,0:T(8,128)(2,1)S(1)}, u32[]{:S(2)}, u32[]{:S(2)}) collective-permute-start(bf16[16,512]{1,0:T(8,128)(2,1)S(1)} %join.1.refs_0_.after), channel_id=1, source_target_pairs={{0,12},{8,0},{4,8},{12,4},{1,13},{9,1},{5,9},{13,5},{2,14},{10,2},... | collective-permute-start | bytes 49160 | tf_op jit(solution)/shard_map/ppermute | solution.py:36
  11.3 3.7 %collective-permute-start.5 = (bf16[16,512]{1,0:T(8,128)(2,1)S(1)}, bf16[16,512]{1,0:T(8,128)(2,1)S(1)}, u32[]{:S(2)}, u32[]{:S(2)}) collective-permute-start(bf16[16,512]{1,0:T(8,128)(2,1)S(1)} %join.1.refs_0_.after), channel_id=1, source_target_pairs={{0,4},{8,12},{4,0},{12,8},{1,5},{9,13},{5,1},{13,9},{2,6},{10,14},... | collective-permute-start | bytes 49160 | tf_op jit(solution)/shard_map/ppermute | solution.py:36
  11.7 9.1 %collective-permute-start.6 = (bf16[16,512]{1,0:T(8,128)(2,1)S(1)}, bf16[16,512]{1,0:T(8,128)(2,1)S(1)}, u32[]{:S(2)}, u32[]{:S(2)}) collective-permute-start(bf16[16,512]{1,0:T(8,128)(2,1)S(1)} %get-tuple-element.32), channel_id=1, source_target_pairs={{0,1},{2,3},{4,5},{6,7},{8,9},{10,11},{12,13},{14,15},{1,0},{3,2},... | collective-permute-start | bytes 49160 | tf_op jit(solution)/shard_map/ppermute | solution.py:42
  11.7 9.1 %collective-permute-start.7 = (bf16[16,512]{1,0:T(8,128)(2,1)S(1)}, bf16[16,512]{1,0:T(8,128)(2,1)S(1)}, u32[]{:S(2)}, u32[]{:S(2)}) collective-permute-start(bf16[16,512]{1,0:T(8,128)(2,1)S(1)} %get-tuple-element.33), channel_id=1, source_target_pairs={{1,2},{3,4},{5,6},{7,8},{9,10},{11,12},{13,14},{15,0},{2,1},{4,3},... | collective-permute-start | bytes 49160 | tf_op jit(solution)/shard_map/ppermute | solution.py:42
  16.6 11.1 %all-to-all-start = ((bf16[16,4,512]{2,1,0:T(4,128)(2,1)}), bf16[16,4,512]{2,1,0:T(4,128)(2,1)S(1)}, u32[]{:S(2)}, u32[]{:S(2)}) async-start(bf16[16,4,512]{2,1,0:T(4,128)(2,1)} %get-tuple-element.29.after), calls=%async_computation | async-start | bytes 131072 | tf_op jit(solution)/shard_map/all_to_all | solution.py:329
